TPU v7x, 256 devices: a whole 4x4x8 slice. The times are simulated.
256 devices in a mesh: dp: 32 (over y, x, core), mp: 8 (over z).
Axes of the slice: x: 4, y: 4, z: 8, core: 2. Of those that a mesh axis runs over, the one named last changes fastest.
Arguments:
- token_keys: bfloat16 [4096, 25600], P('dp', 'mp'), may hold values from -6 to 6
- token_grads: bfloat16 [4096, 5120], P('dp', 'mp'), may hold values from -6 to 6
- prompt_ids: int32 [4096], P('dp'), may hold values from 0 to 511, never falling along the last dimension, each value on 1 to 32 neighbouring positions
- key_weight: bfloat16 [25600, 1024], P('mp'), may hold values from -0.0390625 to 0.0390625
- grad_weight: bfloat16 [5120, 1024], P('mp'), may hold values from -0.078125 to 0.078125
- hidden_bias: float32 [1024], replicated, may hold values from -3 to 3
- gate_vector: float32 [1024], replicated, may hold values from -0.375 to 0.375
- grad_output: bfloat16 [1024, 5120], P(None, 'mp'), may hold values from -0.1875 to 0.1875
- down_weight: bfloat16 [25600, 5120], P('mp', 'dp'), may hold values from -0.0390625 to 0.0390625
- locality_bank: bfloat16 [320, 25600], P(None, 'mp'), may hold values from -6 to 6
- locality_ids: int32 [256], replicated, may hold values from 0 to 319
Outputs:
- locality_out: bfloat16 [256, 5120], P('mp', 'dp')
Inputs may be any that keep to these rules, and one draw needn't show every extreme that they name: prompt_ids never fall along the tokens; every prompt has 1 to 32 tokens and some prompt has exactly 32.
All inputs are finite; a program needn't handle non-finite values.
Results may differ from a plain program's by a relative error of at most 0.024.
Values may be sent and summed in bfloat16 or wider, within the bound.
A program may use at most 128 MiB of HBM per device.

v0:
```python
import jax
import jax.numpy as jnp
from jax import lax
from jax.sharding import PartitionSpec as P

FF = 25600
PROMPT_DEV = 16


def local(
    token_keys,
    token_grads,
    prompt_ids,
    key_weight,
    grad_weight,
    hidden_bias,
    gate_vector,
    grad_output,
    down_weight,
    locality_bank,
    locality_ids,
):
    partial_value = jnp.dot(token_keys, key_weight, preferred_element_type=jnp.float32)
    partial_value = partial_value + jnp.dot(
        token_grads, grad_weight, preferred_element_type=jnp.float32
    )
    pre_act = lax.psum(partial_value.astype(jnp.bfloat16), "mp").astype(jnp.float32)
    hidden = jax.nn.relu(pre_act + hidden_bias).astype(jnp.bfloat16)
    prompt_total = PROMPT_DEV * lax.axis_size("dp")
    onehot = (prompt_ids[:, None] == jnp.arange(prompt_total, dtype=jnp.int32)[None, :]).astype(
        jnp.float32
    )
    counts = lax.psum(jnp.sum(onehot, axis=0), "dp")
    token_count = jnp.dot(onehot, counts, precision=lax.Precision.HIGHEST)
    gate_value = 2.0 * jax.nn.sigmoid(
        jnp.sum(hidden.astype(jnp.float32) * gate_vector[None, :], axis=1)
    )
    weighting = gate_value / token_count
    pseudo_keys = (token_keys.astype(jnp.float32) * weighting[:, None]).astype(jnp.bfloat16)
    pseudo_grads = (
        token_grads.astype(jnp.float32)
        + jnp.dot(hidden, grad_output, preferred_element_type=jnp.float32)
    ).astype(jnp.bfloat16)
    grads_full = lax.all_gather(pseudo_grads, "mp", axis=1, tiled=True)
    locality = jnp.take(locality_bank, locality_ids, axis=0)
    base_term = jnp.dot(locality, down_weight, preferred_element_type=jnp.float32)
    token_total = lax.axis_size("dp") * token_keys.shape[0]
    factor_shift = 4.0 / jnp.sqrt(jnp.float32(FF) * jnp.float32(token_total))
    columns = lax.all_to_all(grads_full, "dp", split_axis=1, concat_axis=0, tiled=True)
    shift = lax.dot_general(
        lax.all_gather(pseudo_keys, "dp", axis=0, tiled=True),
        columns,
        (((0,), (0,)), ((), ())),
        preferred_element_type=jnp.float32,
    )
    total_term = base_term + factor_shift * jnp.dot(
        locality.astype(jnp.float32), shift, precision=lax.Precision.HIGHEST
    )
    result = lax.psum_scatter(
        total_term.astype(jnp.bfloat16), "mp", scatter_dimension=0, tiled=True
    )
    return result


def solution(mesh):
    placed = (
        P("dp", "mp"),
        P("dp", "mp"),
        P("dp"),
        P("mp", None),
        P("mp", None),
        P(),
        P(),
        P(None, "mp"),
        P("mp", "dp"),
        P(None, "mp"),
        P(),
    )
    return jax.shard_map(
        local, mesh=mesh, in_specs=placed, out_specs=P("mp", "dp"), check_vma=False
    )
```

profile of v0, /device:TPU:7, one launch (start us, length us, event | category | flops | bytes accessed | tf_op | source)
XLA Modules:
  0.0 309.5 jit_solution(11422794955709866295)
XLA Ops:
  6.5 0.0 copy-start
  6.5 0.0 all-reduce.2.cloned.1.call-start
  6.5 4.3 %fusion.13 = f32[128,1024]{1,0:T(8,128)S(1)} fusion(bf16[128,3200]{1,0:T(8,128)(2,1)} %param.11, bf16[3200,1024]{1,0:T(8,128)(2,1)} %param.14), kind=kOutput, calls=%fused_computation.27 | convolution fusion | flops 838860800 | bytes 7897088 | tf_op jit(solution)/shard_map/dot_general | solution.py:23
  10.9 0.0 copy-done.5
  10.9 0.0 copy-start.7
  10.9 1.1 fusion.3
  12.0 0.0 all-reduce.2.cloned.1.call-update
  12.0 0.0 all-gather.5.cloned.1.call-start
  12.1 70.9 %all-reduce.2.cloned.1.call-done = bf16[128,1024]{1,0:T(8,128)(2,1)} async-done(((bf16[128,1024]{1,0:T(8,128)(2,1)}), bf16[128,1024]{1,0:T(8,128)(2,1)}) %all-reduce.2.cloned.1.call-update) | async-done | bytes 262160 | tf_op jit(solution)/shard_map/psum | solution.py:27
  83.0 2.5 fusion.5
  85.4 0.0 all-gather.5.cloned.1.call-update
  85.5 0.0 all-gather.3.cloned.1.call-start
  85.5 0.0 copy-done.10
  85.5 0.1 convert_reduce_fusion
  85.6 54.9 %psum.15 = f32[512]{0:T(512)S(1)} all-reduce(f32[512]{0:T(512)S(1)} %convert_reduce_fusion), channel_id=1, replica_groups=mesh['dp'=32,'mp'=8] {'dp'}, use_global_device_ids=true, to_apply=%region_3.4 | all-reduce | flops 512 | bytes 4096 | tf_op jit(solution)/shard_map/psum | solution.py:33
  140.6 0.2 multiply_reduce_fusion
  140.7 0.2 fusion.7
  141.0 0.0 copy-done.2
  141.0 1.2 multiply_convert_fusion
  142.2 0.0 all-gather.3.cloned.1.call-update
  142.2 0.0 all-gather.5.cloned.1.call-done
  142.2 2.4 copy.14
  144.7 16.9 %all-to-all-start = ((bf16[128,32,160]{0,2,1:T(8,128)(2,1)}), bf16[128,32,160]{0,2,1:T(8,128)(2,1)S(1)}, u32[]{:S(2)}, u32[]{:S(2)}) async-start(bf16[128,32,160]{0,2,1:T(8,128)(2,1)} %bitcast.2), calls=%async_computation | async-start | bytes 2621440 | tf_op jit(solution)/shard_map/all_to_all | solution.py:49
  161.6 0.0 reduce-scatter.2.cloned.1.call-start
  161.7 2.9 gather_fusion
  164.5 3.1 fusion.8
  167.6 25.8 %all-to-all-done = bf16[128,32,160]{0,2,1:T(8,128)(2,1)S(1)} async-done(((bf16[128,32,160]{0,2,1:T(8,128)(2,1)}), bf16[128,32,160]{0,2,1:T(8,128)(2,1)S(1)}, u32[]{:S(2)}, u32[]{:S(2)}) %all-to-all-start) | async-done | bytes 1310752 | tf_op jit(solution)/shard_map/all_to_all | solution.py:49
  193.4 65.7 %all-gather.3.cloned.1.call-done = bf16[4096,3200]{1,0:T(8,128)(2,1)} async-done(((bf16[128,3200]{1,0:T(8,128)(2,1)}), bf16[4096,3200]{1,0:T(8,128)(2,1)}) %all-gather.3.cloned.1.call-update) | async-done | bytes 26214416 | tf_op jit(solution)/shard_map/all_gather | solution.py:51
  259.2 11.2 %fusion = f32[3200,160]{0,1:T(8,128)S(1)} fusion(bf16[4096,3200]{1,0:T(8,128)(2,1)} %all-gather.3.cloned.1.call-done, bf16[128,32,160]{0,2,1:T(8,128)(2,1)S(1)} %all-to-all-done), kind=kOutput, calls=%fused_computation.3 | convolution fusion | flops 4194304000 | bytes 29573120 | tf_op jit(solution)/shard_map/dot_general | solution.py:50
  270.4 2.4 fusion.6
  272.7 0.0 reduce-scatter.2.cloned.1.call-update
  272.7 30.2 %reduce-scatter.2.cloned.1.call-done = bf16[32,160]{1,0:T(8,128)(2,1)} async-done(((bf16[256,160]{1,0:T(8,128)(2,1)}), bf16[32,160]{1,0:T(8,128)(2,1)}) %reduce-scatter.2.cloned.1.call-update) | async-done | bytes 10256 | tf_op jit(solution)/shard_map/reduce_scatter | solution.py:59
  (20 shorter events, 0.0 us)
Async XLA Ops:
  6.5 155.1 %copy-start = (bf16[320,3200]{1,0:T(8,128)(2,1)S(1)}, bf16[320,3200]{1,0:T(8,128)(2,1)}, u32[]{:S(2)}) copy-start(bf16[320,3200]{1,0:T(8,128)(2,1)} %param.20) | copy-start | bytes 6144004
  6.5 4.3 %copy-start.5 = (bf16[128,640]{1,0:T(8,128)(2,1)S(1)}, bf16[128,640]{1,0:T(8,128)(2,1)}, u32[]{:S(2)}) copy-start(bf16[128,640]{1,0:T(8,128)(2,1)} %param.12) | copy-start | bytes 491524
  6.5 4.3 %copy-start.3 = (bf16[640,1024]{1,0:T(8,128)(2,1)S(1)}, bf16[640,1024]{1,0:T(8,128)(2,1)}, u32[]{:S(2)}) copy-start(bf16[640,1024]{1,0:T(8,128)(2,1)} %param.15) | copy-start | bytes 3932164
  6.5 76.4 %all-reduce.2.cloned.1.call-start = ((), (), s32[]{:S(2)}) async-start(), calls=%async_computation.2 | async-start | bytes 524288 | tf_op jit(solution)/shard_map/psum | solution.py:27
  10.9 72.1 %copy-start.7 = (f32[1024]{0:T(1024)S(1)}, f32[1024]{0:T(1024)}, u32[]{:S(2)}) copy-start(f32[1024]{0:T(1024)} %param.16) | copy-start | bytes 12292
  12.0 73.5 %copy-start.10 = (s32[128]{0:T(128)S(1)}, s32[128]{0:T(128)}, u32[]{:S(2)}) copy-start(s32[128]{0:T(128)} %param.13) | copy-start | bytes 1540
  12.0 128.6 %copy-start.8 = (f32[1024]{0:T(1024)S(1)}, f32[1024]{0:T(1024)}, u32[]{:S(2)}) copy-start(f32[1024]{0:T(1024)} %param.17) | copy-start | bytes 12292
  12.0 129.0 %copy-start.2 = (bf16[128,3200]{1,0:T(8,128)(2,1)S(1)}, bf16[128,3200]{1,0:T(8,128)(2,1)}, u32[]{:S(2)}) copy-start(bf16[128,3200]{1,0:T(8,128)(2,1)} %param.11) | copy-start | bytes 2457604
  12.0 130.2 %all-gather.5.cloned.1.call-start = ((), (), s32[]{:S(2)}) async-start(), calls=%async_computation.4 | async-start | bytes 1474560 | tf_op jit(solution)/shard_map/all_gather | solution.py:44
  83.0 57.6 %copy-start.4 = (bf16[128,1024]{1,0:T(8,128)(2,1)S(1)}, bf16[128,1024]{1,0:T(8,128)(2,1)}, u32[]{:S(2)}) copy-start(bf16[128,1024]{1,0:T(8,128)(2,1)} %all-reduce.2.cloned.1.call-done) | copy-start | bytes 786436
  85.5 173.7 %all-gather.3.cloned.1.call-start = ((), (), s32[]{:S(2)}) async-start(), calls=%async_computation.3 | async-start | bytes 27033600 | tf_op jit(solution)/shard_map/all_gather | solution.py:51
  144.7 17.0 %copy-start.9 = (s32[256]{0:T(256)S(1)}, s32[256]{0:T(256)}, u32[]{:S(2)}) copy-start(s32[256]{0:T(256)} %param.21) | copy-start | bytes 3076
  144.7 48.8 %all-to-all-start = ((bf16[128,32,160]{0,2,1:T(8,128)(2,1)}), bf16[128,32,160]{0,2,1:T(8,128)(2,1)S(1)}, u32[]{:S(2)}, u32[]{:S(2)}) async-start(bf16[128,32,160]{0,2,1:T(8,128)(2,1)} %bitcast.2), calls=%async_computation | async-start | bytes 2621440 | tf_op jit(solution)/shard_map/all_to_all | solution.py:49
  161.6 141.4 %reduce-scatter.2.cloned.1.call-start = ((), (), s32[]{:S(2)}) async-start(), calls=%async_computation.5 | async-start | bytes 147456 | tf_op jit(solution)/shard_map/reduce_scatter | solution.py:59
  259.2 11.2 %copy-start.1 = (bf16[256,3200]{1,0:T(8,128)(2,1)S(1)}, bf16[256,3200]{1,0:T(8,128)(2,1)}, u32[]{:S(2)}) copy-start(bf16[256,3200]{1,0:T(8,128)(2,1)} %gather_fusion) | copy-start | bytes 4915204
  259.2 11.2 %copy-start.6 = (f32[256,160]{1,0:T(8,128)S(1)}, f32[256,160]{1,0:T(8,128)}, u32[]{:S(2)}) copy-start(f32[256,160]{1,0:T(8,128)} %fusion.8) | copy-start | bytes 491524
Sparse Core Ops, SparseCore 0:
  12.1 70.7 all-reduce.1
  85.6 37.7 all-gather.4
  142.3 116.7 all-gather.2
  272.9 30.0 reduce-scatter.1
where the time goes:
time: 315 us; the launch traced here: 309 us
  waiting for transfers between devices  193 us (61%)
  blocking collectives  54.9 us (17%)
  matrix products  24.7 us (8%)
  starting transfers between devices  17 us (5%)
  between operations  13.3 us (4%)
  local copies, waits for them, and re-layouts  5.34 us (2%)
    psum x1, waiting for transfers between devices, local(): lax.psum(partial_value.astype(jnp.bfloat16), 'mp').astype(jnp.float32)  70.9 us
    all_gather x1, waiting for transfers between devices, local(): lax.all_gather(pseudo_keys, 'dp', axis=0, tiled=True)  65.7 us
    psum x1, blocking collectives, local(): counts = lax.psum(jnp.sum(onehot, axis=0), 'dp')  54.9 us
    reduce_scatter x1, waiting for transfers between devices, local(): lax.psum_scatter(total_term.astype(jnp.bfloat16), 'mp', scatter_dimension...  30.2 us
    all_to_all x1, waiting for transfers between devices, local(): lax.all_to_all(grads_full, 'dp', split_axis=1, concat_axis=0, tiled=True)  25.8 us
    all_to_all x1, starting transfers between devices, local(): lax.all_to_all(grads_full, 'dp', split_axis=1, concat_axis=0, tiled=True)  16.9 us
    dot_general x1, matrix products, local(): lax.dot_general(lax.all_gather(pseudo_keys, 'dp', axis=0, tiled=True), co...  11.2 us
  transfers between devices with their start and end apart: 5, of which 4 were waited for; matrix products, arithmetic and copies ran while one was open for 3% of the time, Pallas kernels for 0%

commit v1 on v0

v1 whole, which is shorter than its diff:
```python
import jax
import jax.numpy as jnp
from jax import lax
from jax.sharding import PartitionSpec as P

FF = 25600


def local(
    token_keys,
    token_grads,
    prompt_ids,
    key_weight,
    grad_weight,
    hidden_bias,
    gate_vector,
    grad_output,
    down_weight,
    locality_bank,
    locality_ids,
):
    n_dp, n_mp = lax.axis_size("dp"), lax.axis_size("mp")
    rows = locality_ids.shape[0]
    locality = jnp.take(locality_bank, locality_ids, axis=0)
    base_term = jnp.dot(locality, down_weight, preferred_element_type=jnp.float32)
    scores = lax.dot_general(
        token_keys, locality, (((1,), (1,)), ((), ())), preferred_element_type=jnp.float32
    )
    partial_value = jnp.dot(token_keys, key_weight, preferred_element_type=jnp.float32)
    partial_value = partial_value + jnp.dot(
        token_grads, grad_weight, preferred_element_type=jnp.float32
    )
    both = jnp.concatenate([partial_value, scores], axis=1).astype(jnp.bfloat16)
    both = lax.psum(both, "mp")
    width = partial_value.shape[1]
    pre_act = both[:, :width].astype(jnp.float32)
    scores = both[:, width:]
    hidden = jax.nn.relu(pre_act + hidden_bias).astype(jnp.bfloat16)
    left = lax.ppermute(prompt_ids, "dp", [(i, (i + 1) % n_dp) for i in range(n_dp)])
    right = lax.ppermute(prompt_ids, "dp", [(i, (i - 1) % n_dp) for i in range(n_dp)])
    near = jnp.concatenate([left, prompt_ids, right])
    token_count = jnp.sum((prompt_ids[:, None] == near[None, :]).astype(jnp.float32), axis=1)
    gate_value = 2.0 * jax.nn.sigmoid(
        jnp.sum(hidden.astype(jnp.float32) * gate_vector[None, :], axis=1)
    )
    weighting = gate_value / token_count
    pseudo_grads = token_grads.astype(jnp.float32) + jnp.dot(
        hidden, grad_output, preferred_element_type=jnp.float32
    )
    weighted = (pseudo_grads * weighting[:, None]).astype(jnp.bfloat16)
    spread = lax.dot_general(
        scores, weighted, (((0,), (0,)), ((), ())), preferred_element_type=jnp.float32
    ).astype(jnp.bfloat16)
    cols = n_dp // n_mp
    high, wide = rows // n_mp, spread.shape[1] // cols
    blocks = spread.reshape(n_mp, high, cols, wide).transpose(0, 2, 1, 3).reshape(n_dp, high, wide)
    mine = lax.psum_scatter(blocks, "dp", scatter_dimension=0, tiled=True)[0]
    pairs = []
    for d in range(n_dp):
        for m in range(n_mp):
            pairs.append((d * n_mp + m, (m * cols + d % cols) * n_mp + d // cols))
    mine = lax.ppermute(mine, ("dp", "mp"), pairs).astype(jnp.float32)
    base = lax.psum_scatter(
        base_term.astype(jnp.bfloat16), "mp", scatter_dimension=0, tiled=True
    ).astype(jnp.float32)
    token_total = n_dp * token_keys.shape[0]
    factor_shift = 4.0 / jnp.sqrt(jnp.float32(FF) * jnp.float32(token_total))
    return (base + factor_shift * mine).astype(jnp.bfloat16)


def solution(mesh):
    placed = (
        P("dp", "mp"),
        P("dp", "mp"),
        P("dp"),
        P("mp", None),
        P("mp", None),
        P(),
        P(),
        P(None, "mp"),
        P("mp", "dp"),
        P(None, "mp"),
        P(),
    )
    return jax.shard_map(
        local, mesh=mesh, in_specs=placed, out_specs=P("mp", "dp"), check_vma=False
    )
```

time: 315 us -> 229 us (0.73)
  the two profiles are of different devices: /device:TPU:7 before, /device:TPU:6 now
where the time goes in v1:
time: 229 us
  waiting for transfers between devices  188 us (82%)
  between operations  13.3 us (6%)
  matrix products  11.9 us (5%)
  starting transfers between devices  6.27 us (3%)
  other arithmetic  5.46 us (2%)
  local copies, waits for them, and re-layouts  4.15 us (2%)
    reduce_scatter x1, waiting for transfers between devices, local(): mine = lax.psum_scatter(blocks, 'dp', scatter_dimension=0, tiled=True)[0]  79.7 us
    psum x1, waiting for transfers between devices, local(): both = lax.psum(both, 'mp')  72.4 us
    reduce_scatter x1, waiting for transfers between devices, local(): lax.psum_scatter(base_term.astype(jnp.bfloat16), 'mp', scatter_dimension=...  34.6 us
  transfers between devices with their start and end apart: 6, of which 5 were waited for; matrix products, arithmetic and copies ran while one was open for 1% of the time, Pallas kernels for 0%

profile of v1, /device:TPU:6, one launch (start us, length us, event | category | flops | bytes accessed | tf_op | source)
XLA Modules:
  0.0 229.1 jit_solution(348556768278141016)
XLA Ops:
  6.5 1.3 compare_and_fusion
  7.9 0.7 compare_select_fusion
  8.6 4.2 %fusion.11 = f32[128,1024]{1,0:T(8,128)S(1)} fusion(bf16[128,3200]{1,0:T(8,128)(2,1)} %param.11, bf16[3200,1024]{1,0:T(8,128)(2,1)} %param.14), kind=kOutput, calls=%fused_computation.27 | convolution fusion | flops 838860800 | bytes 7897088 | tf_op jit(solution)/shard_map/dot_general | solution.py:29
  12.8 0.0 copy-start.2
  12.8 2.9 %gather_fusion = bf16[256,3200]{1,0:T(8,128)(2,1)} fusion(bf16[320,3200]{1,0:T(8,128)(2,1)S(1)} %copy-done, s32[1024]{0:T(1024)S(1)} %pad_clamp_fusion), kind=kCustom, calls=%fused_computation | custom fusion | bytes 3277824 | tf_op jit(solution)/shard_map/jit(_take)/gather | solution.py:24
  15.7 2.3 fusion.3
  18.0 0.0 copy-start.6
  18.0 0.0 copy-start.4
  18.0 0.0 copy-start.5
  18.0 0.4 fusion
  18.4 0.8 pad_maximum_fusion
  19.2 0.0 all-reduce.2.cloned.1.call-update
  19.2 0.0 reduce-scatter.5.cloned.1.call-start
  19.3 0.1 collective-permute-start
  19.3 1.7 collective-permute-start.1
  21.1 1.2 collective-permute-done
  22.3 0.1 collective-permute-done.1
  22.4 0.2 convert_reduce_fusion
  22.6 72.4 %all-reduce.2.cloned.1.call-done = bf16[128,1280]{1,0:T(8,128)(2,1)} async-done(((bf16[128,1280]{1,0:T(8,128)(2,1)}), bf16[128,1280]{1,0:T(8,128)(2,1)}) %all-reduce.2.cloned.1.call-update) | async-done | bytes 327696 | tf_op jit(solution)/shard_map/psum | solution.py:34
  95.0 1.1 multiply_reduce_fusion
  96.1 2.0 convolution_convert_fusion
  98.2 0.0 copy-start.7
  98.2 0.4 reshape.25
  98.6 0.9 copy.15
  99.5 0.0 reduce-scatter.5.cloned.1.call-update
  99.5 0.0 reduce-scatter.3.cloned.1.call-start
  99.5 3.0 %convolution_convert_fusion.1 = bf16[256,160]{1,0:T(8,128)(2,1)} fusion(bf16[3200,160]{0,1:T(8,128)(2,1)} %param.19, bf16[256,3200]{1,0:T(8,128)(2,1)} %gather_fusion, pred[256]{0:T(512)(128)(4,1)S(1)} %copy-done.7), kind=kOutput, calls=%fused_computation.8 | convolution fusion | flops 263004160 | bytes 2744576 | tf_op jit(solution)/shard_map/dot_general | solution.py:25
  102.6 0.0 reduce-scatter.3.cloned.1.call-update
  102.6 79.7 %reduce-scatter.5.cloned.1.call-done = bf16[1,32,160]{2,1,0:T(8,128)(2,1)} async-done(((bf16[32,32,160]{2,1,0:T(8,128)(2,1)}), bf16[1,32,160]{2,1,0:T(8,128)(2,1)}) %reduce-scatter.5.cloned.1.call-update) | async-done | bytes 10256 | tf_op jit(solution)/shard_map/reduce_scatter | solution.py:57
  182.3 4.4 %collective-permute-start.2 = (bf16[32,160]{1,0:T(8,128)(2,1)}, bf16[32,160]{1,0:T(8,128)(2,1)S(1)}, u32[]{:S(2)}, u32[]{:S(2)}) collective-permute-start(bf16[32,160]{1,0:T(8,128)(2,1)} %bitcast.14), channel_id=1, source_target_pairs={{0,0},{1,32},{2,64},{3,96},{4,128},{5,160},{6,192},{7,224},{8,8},{... | collective-permute-start | bytes 30728 | tf_op jit(solution)/shard_map/ppermute | solution.py:62
  186.7 34.6 %reduce-scatter.3.cloned.1.call-done = bf16[32,160]{1,0:T(8,128)(2,1)} async-done(((bf16[256,160]{1,0:T(8,128)(2,1)}), bf16[32,160]{1,0:T(8,128)(2,1)}) %reduce-scatter.3.cloned.1.call-update) | async-done | bytes 10256 | tf_op jit(solution)/shard_map/reduce_scatter | solution.py:63
  221.3 1.3 add_convert_fusion
  (16 shorter events, 0.1 us)
Async XLA Ops:
  6.5 6.2 %copy-start = (bf16[320,3200]{1,0:T(8,128)(2,1)S(1)}, bf16[320,3200]{1,0:T(8,128)(2,1)}, u32[]{:S(2)}) copy-start(bf16[320,3200]{1,0:T(8,128)(2,1)} %param.20) | copy-start | bytes 6144004
  6.5 88.5 %all-reduce.2.cloned.1.call-start = ((), (), s32[]{:S(2)}) async-start(), calls=%async_computation.3 | async-start | bytes 655360 | tf_op jit(solution)/shard_map/psum | solution.py:34
  12.8 2.9 %copy-start.2 = (bf16[128,3200]{1,0:T(8,128)(2,1)S(1)}, bf16[128,3200]{1,0:T(8,128)(2,1)}, u32[]{:S(2)}) copy-start(bf16[128,3200]{1,0:T(8,128)(2,1)} %param.11) | copy-start | bytes 2457604
  15.6 2.3 %copy-start.1 = (bf16[640,1024]{1,0:T(8,128)(2,1)S(1)}, bf16[640,1024]{1,0:T(8,128)(2,1)}, u32[]{:S(2)}) copy-start(bf16[640,1024]{1,0:T(8,128)(2,1)} %param.15) | copy-start | bytes 3932164
  15.6 2.3 %copy-start.3 = (bf16[128,640]{1,0:T(8,128)(2,1)S(1)}, bf16[128,640]{1,0:T(8,128)(2,1)}, u32[]{:S(2)}) copy-start(bf16[128,640]{1,0:T(8,128)(2,1)} %param.12) | copy-start | bytes 491524
  18.0 1.3 copy-start.6
  18.0 77.0 %copy-start.4 = (f32[1024]{0:T(1024)S(1)}, f32[1024]{0:T(1024)}, u32[]{:S(2)}) copy-start(f32[1024]{0:T(1024)} %param.17) | copy-start | bytes 12292
  18.0 77.0 %copy-start.5 = (f32[1024]{0:T(1024)S(1)}, f32[1024]{0:T(1024)}, u32[]{:S(2)}) copy-start(f32[1024]{0:T(1024)} %param.16) | copy-start | bytes 12292
  19.2 163.1 %reduce-scatter.5.cloned.1.call-start = ((), (), s32[]{:S(2)}) async-start(), calls=%async_computation.4 | async-start | bytes 540672 | tf_op jit(solution)/shard_map/reduce_scatter | solution.py:57
  19.3 3.0 %collective-permute-start = (s32[128]{0:T(128)S(1)}, s32[128]{0:T(128)S(1)}, u32[]{:S(2)}, u32[]{:S(2)}) collective-permute-start(s32[128]{0:T(128)S(1)} %copy-done.6), channel_id=1, source_target_pairs={{0,8},{8,16},{16,24},{24,32},{32,40},{40,48},{48,56},{56,64},{64,7... | collective-permute-start | bytes 1544 | tf_op jit(solution)/shard_map/ppermute | solution.py:39
  19.3 3.0 %collective-permute-start.1 = (s32[128]{0:T(128)S(1)}, s32[128]{0:T(128)S(1)}, u32[]{:S(2)}, u32[]{:S(2)}) collective-permute-start(s32[128]{0:T(128)S(1)} %copy-done.6), channel_id=1, source_target_pairs={{0,248},{8,0},{16,8},{24,16},{32,24},{40,32},{48,40},{56,48},{64,5... | collective-permute-start | bytes 1544 | tf_op jit(solution)/shard_map/ppermute | solution.py:40
  98.2 1.3 copy-start.7
  99.5 121.8 %reduce-scatter.3.cloned.1.call-start = ((), (), s32[]{:S(2)}) async-start(), calls=%async_computation.2 | async-start | bytes 147456 | tf_op jit(solution)/shard_map/reduce_scatter | solution.py:63
  182.3 38.9 %collective-permute-start.2 = (bf16[32,160]{1,0:T(8,128)(2,1)}, bf16[32,160]{1,0:T(8,128)(2,1)S(1)}, u32[]{:S(2)}, u32[]{:S(2)}) collective-permute-start(bf16[32,160]{1,0:T(8,128)(2,1)} %bitcast.14), channel_id=1, source_target_pairs={{0,0},{1,32},{2,64},{3,96},{4,128},{5,160},{6,192},{7,224},{8,8},{... | collective-permute-start | bytes 30728 | tf_op jit(solution)/shard_map/ppermute | solution.py:62
Sparse Core Ops, SparseCore 0:
  19.3 75.6 all-reduce.1
  99.6 82.6 reduce-scatter.4
  185.0 36.2 reduce-scatter.2

commit v2 on v0

v2 whole, which is shorter than its diff:
```python
import jax
import jax.numpy as jnp
from jax import lax
from jax.experimental import pallas as pl
from jax.experimental.pallas import tpu as pltpu
from jax.sharding import PartitionSpec as P

MESH = pl.DeviceIdType.MESH
F32, BF16 = jnp.float32, jnp.bfloat16
NZ, NX, NY, NCHIP = 8, 4, 4, 16
TOK, KEYS, GRADS, HID, ROWS, BANK, COLS = 128, 3200, 640, 1024, 256, 320, 160
TB = TOK // NZ
RB = ROWS // NCHIP
HALF = HID // 2
WIDE = 384
CH = 256
NCH = HID // CH
OB = ROWS // NZ
SCALE = 4.0 / 10240.0

TN = (((0,), (0,)), ((), ()))
NT = (((1,), (1,)), ((), ()))


def kernel(
    tk_h, tg_h, ids_h, kw_h, gw_h, bias_h, gate_h, go_h, dw_h, bank_h, lids_h,
    out_ref,
    tk, tg, ids, kw, gw, bias, gate, go, dw, bank, lids,
    near, pbuf, rz, bbuf, br, hid, swt, uh_tx, uh_rx, uh_sum, uh_rs, ug_tx, ug_rx, ug_sum, ug_rs,
    uz_tx, uz, mm, ftx, frx,
    lsem, kwsem, rz_s, rz_r, b_s, b_r, i_s, i_r, a_s, a_r, c_s, c_r, x_s, x_r, z_s, z_r, f_s, f_r,
):
    d, m = lax.axis_index("dp"), lax.axis_index("mp")
    c = lax.rem(d, 2)
    q = lax.div(d, 2)
    y, x = lax.div(q, NX), lax.rem(q, NX)
    sibling = (d + 1 - 2 * c, m)

    def zdev(k):
        return (d, lax.rem(m + k, NZ))

    def chip(k):
        ky, kx = divmod(k, NX)
        return lax.rem(y + ky, NY) * NX + lax.rem(x + kx, NX)

    def rows_of(chip_index):
        return pl.ds(pl.multiple_of(lax.rem(chip_index + NCHIP // 2, NCHIP) * RB, RB), RB)

    def remote(src, dst, s, r, dev):
        pltpu.make_async_remote_copy(
            src_ref=src, dst_ref=dst, send_sem=s, recv_sem=r, device_id=dev, device_id_type=MESH
        ).start()

    def await_bytes(buf, sem):
        pltpu.make_async_copy(buf, buf, sem).wait()

    core_rows = pl.ds(pl.multiple_of(c * HALF, HALF), HALF)
    loads = dict(
        tk=(tk_h, tk), bank=(bank_h, bank), lids=(lids_h, lids), tg=(tg_h, tg), gw=(gw_h, gw),
        ids=(ids_h, ids), bias=(bias_h, bias), gate=(gate_h, gate),
        dw=(dw_h, dw), go=(go_h.at[core_rows], go),
    )
    number = {name: i for i, name in enumerate(loads)}

    def load(name):
        src, dst = loads[name]
        return pltpu.make_async_copy(src, dst, lsem.at[number[name]])

    def load_kw(ch):
        return pltpu.make_async_copy(kw_h.at[:, pl.ds(ch * CH, CH)], kw.at[ch], kwsem.at[ch])

    for name in ("tk", "bank", "lids", "ids", "tg", "gw"):
        load(name).start()
    for ch in range(NCH):
        load_kw(ch).start()
    for name in ("bias", "gate", "dw", "go"):
        load(name).start()

    barrier = pltpu.get_barrier_semaphore()
    beside = [lax.rem(d + 1, 2 * NCHIP), lax.rem(d + 2 * NCHIP - 1, 2 * NCHIP)]
    target = lax.rem(lax.div(d, 4) + NZ // 2, NZ)
    greet = [sibling] + [(e, m) for e in beside]
    greet += [zdev(k) for k in range(1, NZ)]
    greet += [(chip(k) * 2 + c, m) for k in range(1, NCHIP)]
    greet += [(4 * lax.rem(m + NZ // 2, NZ) + s, lax.div(d, 4)) for s in range(4)]
    for dev in greet:
        pl.semaphore_signal(barrier, inc=1, device_id=dev, device_id_type=MESH)

    load("lids").wait()
    ids_row = lids[...].astype(F32)
    pick_t = (
        lax.broadcasted_iota(jnp.int32, (BANK, ROWS), 0).astype(F32) == ids_row
    ).astype(F32).astype(BF16)
    load("tk").wait()
    load("bank").wait()
    bank_scores = lax.dot_general(tk[...], bank[...], NT, preferred_element_type=F32).astype(BF16)
    pbuf[NCH] = jnp.dot(bank_scores, pick_t, preferred_element_type=F32).astype(BF16)
    load("tg").wait()
    load("gw").wait()

    def partial_sum(ch):
        load_kw(ch).wait()
        value = jnp.dot(tk[...], kw[ch], preferred_element_type=F32)
        value = value + jnp.dot(
            tg[...], gw[:, ch * CH:(ch + 1) * CH], preferred_element_type=F32
        )
        pbuf[ch] = value.astype(BF16)

    def send_partial(ch):
        for k in range(1, NZ):
            to = lax.rem(m + k, NZ)
            rows = pl.ds(pl.multiple_of(to * TB, TB), TB)
            remote(pbuf.at[ch, rows], rz.at[ch, k - 1], rz_s.at[ch], rz_r.at[ch], (d, to))

    partial_sum(0)
    load("ids").wait()
    pl.semaphore_wait(barrier, len(greet))
    send_partial(0)
    send_partial(NCH)
    for i, e in enumerate(beside):
        remote(ids, near.at[i], i_s.at[i], i_r.at[i], (e, m))
    for ch in range(1, NCH):
        partial_sum(ch)
        send_partial(ch)

    load("dw").wait()
    square = lax.broadcasted_iota(jnp.int32, (ROWS, ROWS), 0) == lax.broadcasted_iota(
        jnp.int32, (ROWS, ROWS), 1
    )
    ids_col = jnp.sum(jnp.where(square, jnp.broadcast_to(ids_row, (ROWS, ROWS)), 0.0), axis=1, keepdims=True)
    pick = (
        lax.broadcasted_iota(jnp.int32, (ROWS, BANK), 1).astype(F32) == ids_col
    ).astype(F32).astype(BF16)
    bank_down = lax.dot_general(bank[...], dw[...], NT, preferred_element_type=F32).astype(BF16)
    bbuf[...] = jnp.dot(pick, bank_down, preferred_element_type=F32).astype(BF16)
    for k in range(1, NZ):
        to = lax.rem(m + k, NZ)
        remote(
            bbuf.at[pl.ds(pl.multiple_of(to * OB, OB), OB)], br.at[k - 1], b_s.at[0], b_r.at[0], (d, to)
        )

    own_ids = ids[...].astype(F32)
    wanted = lax.broadcasted_iota(jnp.int32, (TB, TOK), 1) == (
        lax.broadcasted_iota(jnp.int32, (TB, TOK), 0) + m * TB
    )
    ids_here = jnp.sum(jnp.where(wanted, jnp.broadcast_to(own_ids, (TB, TOK)), 0.0), axis=1, keepdims=True)
    count = jnp.sum((ids_here == own_ids).astype(F32), axis=1, keepdims=True)
    for i in range(2):
        pltpu.make_async_copy(ids, near.at[i], i_r.at[i]).wait()
        count = count + jnp.sum((ids_here == near[i].astype(F32)).astype(F32), axis=1, keepdims=True)

    load("bias").wait()
    load("gate").wait()
    mine = pl.ds(pl.multiple_of(m * TB, TB), TB)

    def summed(ch):
        await_bytes(rz.at[ch], rz_r.at[ch])
        value = pbuf[ch, mine].astype(F32)
        for k in range(NZ - 1):
            value = value + rz[ch, k].astype(F32)
        return value

    gated = jnp.zeros((TB, 1), F32)
    for ch in range(NCH):
        cut = slice(ch * CH, (ch + 1) * CH)
        hidden = jnp.maximum(summed(ch) + bias[:, cut], 0.0).astype(BF16)
        hid[:, cut] = hidden
        gated = gated + jnp.sum(hidden.astype(F32) * gate[:, cut], axis=1, keepdims=True)
    weight = 2.0 / ((1.0 + jnp.exp(-gated)) * count)
    sw = (summed(NCH) * weight).astype(BF16)
    swt[mine] = sw
    for k in range(1, NZ):
        remote(swt.at[mine], swt.at[mine], a_s.at[0], a_r.at[0], zdev(k))

    def half(core):
        return pl.ds(pl.multiple_of(core * HALF, HALF), HALF)

    uh_tx[...] = lax.dot_general(sw, hid[:, half(1 - c)], TN, preferred_element_type=F32).astype(BF16)
    remote(uh_tx, uh_rx, c_s.at[0], c_r.at[0], sibling)
    own = lax.dot_general(sw, hid[:, half(c)], TN, preferred_element_type=F32)
    await_bytes(uh_rx, c_r.at[0])
    uh_sum[...] = (own + uh_rx[...].astype(F32)).astype(BF16)
    for k in range(1, NCHIP):
        to = chip(k)
        remote(uh_sum.at[rows_of(to)], uh_rs.at[k - 1], x_s.at[0], x_r.at[0], (to * 2 + c, m))

    def window(core):
        return pl.ds(pl.multiple_of(core * 256, 256), WIDE)

    await_bytes(swt.at[pl.ds(0, TOK - TB)], a_r.at[0])
    scores = swt[...]
    ug_tx[...] = lax.dot_general(scores, tg[:, window(1 - c)], TN, preferred_element_type=F32).astype(BF16)
    remote(ug_tx, ug_rx, c_s.at[1], c_r.at[1], sibling)
    own = lax.dot_general(scores, tg[:, window(c)], TN, preferred_element_type=F32)
    await_bytes(ug_rx, c_r.at[1])
    ug_sum[...] = (own + ug_rx[...].astype(F32)).astype(BF16)
    for k in range(1, NCHIP):
        to = chip(k)
        remote(ug_sum.at[rows_of(to)], ug_rs.at[k - 1], x_s.at[1], x_r.at[1], (to * 2 + c, m))

    await_bytes(uh_rs, x_r.at[0])
    value = uh_sum[rows_of(q)].astype(F32)
    for k in range(NCHIP - 1):
        value = value + uh_rs[k].astype(F32)
    uz_tx[...] = value.astype(BF16)
    for k in range(1, NZ):
        remote(uz_tx, uz.at[k - 1], z_s.at[0], z_r.at[0], zdev(k))

    await_bytes(ug_rs, x_r.at[1])
    grads_part = ug_sum[rows_of(q)].astype(F32)
    for k in range(NCHIP - 1):
        grads_part = grads_part + ug_rs[k].astype(F32)
    lane = lax.broadcasted_iota(jnp.int32, (RB, WIDE), 1)
    grads_part = jnp.where(lane >= c * 128, grads_part, 0.0)

    load("go").wait()
    await_bytes(uz, z_r.at[0])
    for k in range(NZ - 1):
        value = value + uz[k].astype(F32)
    mm[...] = jnp.dot(value.astype(BF16), go[...], preferred_element_type=F32)
    mm[:, window(c)] = mm[:, window(c)] + grads_part
    ftx[...] = mm[...].astype(BF16)
    slot = lax.rem(d, 4)
    for j in range(4):
        remote(ftx.at[:, pl.ds(128 * j, 256)], frx.at[slot], f_s.at[0], f_r.at[0], (4 * m + j, target))

    await_bytes(br, b_r.at[0])
    base = bbuf[pl.ds(pl.multiple_of(m * OB, OB), OB)].astype(F32)
    for k in range(NZ - 1):
        base = base + br[k].astype(F32)
    await_bytes(frx, f_r.at[0])
    spread = jnp.concatenate(
        [frx[0].astype(F32) + frx[1].astype(F32), frx[2].astype(F32) + frx[3].astype(F32)], axis=0
    )
    spread = pltpu.roll(spread, lax.rem(256 - 32 * slot, 256), 1)
    out_ref[...] = (base + SCALE * spread[:, :COLS]).astype(BF16)

    for ch in range(NCH + 1):
        await_bytes(rz.at[ch], rz_s.at[ch])
    await_bytes(br, b_s.at[0])
    for i in range(2):
        pltpu.make_async_copy(ids, near.at[i], i_s.at[i]).wait()
    await_bytes(swt.at[pl.ds(0, TOK - TB)], a_s.at[0])
    await_bytes(uh_rx, c_s.at[0])
    await_bytes(ug_rx, c_s.at[1])
    await_bytes(uh_rs, x_s.at[0])
    await_bytes(ug_rs, x_s.at[1])
    await_bytes(uz, z_s.at[0])
    await_bytes(frx, f_s.at[0])


def local(
    token_keys, token_grads, prompt_ids, key_weight, grad_weight, hidden_bias, gate_vector, grad_output,
    down_weight, locality_bank, locality_ids,
):
    vm = pltpu.VMEM
    dma = pltpu.SemaphoreType.DMA
    scratch = [
        vm((TOK, KEYS), BF16), vm((TOK, GRADS), BF16), vm((1, TOK), jnp.int32),
        vm((NCH, KEYS, CH), BF16), vm((GRADS, HID), BF16), vm((1, HID), F32), vm((1, HID), F32),
        vm((HALF, GRADS), BF16), vm((COLS, KEYS), BF16), vm((BANK, KEYS), BF16), vm((1, ROWS), jnp.int32),
        vm((2, 1, TOK), jnp.int32),
        vm((NCH + 1, TOK, CH), BF16), vm((NCH + 1, NZ - 1, TB, CH), BF16),
        vm((ROWS, COLS), BF16), vm((NZ - 1, OB, COLS), BF16),
        vm((TB, HID), BF16), vm((TOK, ROWS), BF16),
        vm((ROWS, HALF), BF16), vm((ROWS, HALF), BF16), vm((ROWS, HALF), BF16),
        vm((NCHIP - 1, RB, HALF), BF16),
        vm((ROWS, WIDE), BF16), vm((ROWS, WIDE), BF16), vm((ROWS, WIDE), BF16),
        vm((NCHIP - 1, RB, WIDE), BF16),
        vm((RB, HALF), BF16), vm((NZ - 1, RB, HALF), BF16),
        vm((RB, GRADS), F32), vm((RB, GRADS), BF16), vm((4, RB, 256), BF16),
        dma((10,)), dma((NCH,)), dma((NCH + 1,)), dma((NCH + 1,)), dma((1,)), dma((1,)), dma((2,)), dma((2,)),
        dma((1,)), dma((1,)), dma((2,)), dma((2,)), dma((2,)), dma((2,)), dma((1,)), dma((1,)), dma((1,)), dma((1,)),
    ]
    any_spec = pl.BlockSpec(memory_space=pl.ANY)
    return pl.pallas_call(
        kernel,
        out_shape=jax.ShapeDtypeStruct((OB, COLS), BF16),
        in_specs=[any_spec] * 11,
        out_specs=pl.BlockSpec(memory_space=pltpu.VMEM),
        scratch_shapes=scratch,
        compiler_params=pltpu.CompilerParams(
            collective_id=0, has_side_effects=True, vmem_limit_bytes=60 * 1024 * 1024
        ),
        cost_estimate=pl.CostEstimate(flops=2_000_000_000, bytes_accessed=14_000_000, transcendentals=16),
    )(
        token_keys, token_grads, prompt_ids.reshape(1, TOK), key_weight, grad_weight,
        hidden_bias.reshape(1, HID), gate_vector.reshape(1, HID), grad_output, down_weight.T, locality_bank,
        locality_ids.reshape(1, ROWS),
    )


def solution(mesh):
    placed = (
        P("dp", "mp"), P("dp", "mp"), P("dp"), P("mp", None), P("mp", None), P(), P(), P(None, "mp"),
        P("mp", "dp"), P(None, "mp"), P(),
    )
    return jax.shard_map(
        local, mesh=mesh, in_specs=placed, out_specs=P("mp", "dp"), check_vma=False
    )
```

time: 315 us -> 43.7 us (0.14); the launches traced: 309 us -> 43.5 us
  waiting for transfers between devices: 193 us -> 0 us
  blocking collectives: 54.9 us -> 0 us
  Pallas kernels: 0 us -> 42.2 us
  matrix products: 24.7 us -> 0 us
  starting transfers between devices: 17 us -> 0 us
  between operations: 13.3 us -> 0.01 us
  local copies, waits for them, and re-layouts: 5.34 us -> 1.32 us
    psum x1 -> x0, waiting for transfers between devices: 70.9 us -> none  [local(): lax.psum(partial_value.astype(jnp.bfloat16), 'mp').astype(jnp.float32)]
    all_gather x2 -> x0, waiting for transfers between devices: 65.7 us -> none  [the longest x1 65.7 us: local(): lax.all_gather(pseudo_keys, 'dp', axis=0, tiled=True)]
    psum x1 -> x0, blocking collectives: 54.9 us -> none  [local(): counts = lax.psum(jnp.sum(onehot, axis=0), 'dp')]
    pallas_call x0 -> x1, Pallas kernels: none -> 42.2 us  [local(): pl.pallas_call(kernel, out_shape=jax.ShapeDtypeStruct((OB, COLS), BF16),...]
    reduce_scatter x1 -> x0, waiting for transfers between devices: 30.2 us -> none  [local(): lax.psum_scatter(total_term.astype(jnp.bfloat16), 'mp', scatter_dimension...]
    all_to_all x1 -> x0, waiting for transfers between devices: 25.8 us -> none  [local(): lax.all_to_all(grads_full, 'dp', split_axis=1, concat_axis=0, tiled=True)]
    dot_general x7 -> x0, matrix products: 24.7 us -> none  [the longest x1 11.2 us: local(): lax.dot_general(lax.all_gather(pseudo_keys, 'dp', axis=0, tiled=True), co...]
    all_to_all x1 -> x0, starting transfers between devices: 16.9 us -> none  [local(): lax.all_to_all(grads_full, 'dp', split_axis=1, concat_axis=0, tiled=True)]
  transfers between devices with their start and end apart: 5 -> 0, of which waited for: 4 -> 0; matrix products, arithmetic and copies ran while one was open for 3% -> 0% of each run, Pallas kernels for 0% -> 0%
where the time goes in v2:
time: 43.7 us; the launch traced here: 43.5 us
  Pallas kernels  42.2 us (97%)
  local copies, waits for them, and re-layouts  1.32 us (3%)
    pallas_call x1, Pallas kernels, local(): pl.pallas_call(kernel, out_shape=jax.ShapeDtypeStruct((OB, COLS), BF16),...  42.2 us
    unnamed x1, local copies, waits for them, and re-layouts  1.32 us

profile of v2, /device:TPU:7, one launch (start us, length us, event | category | flops | bytes accessed | tf_op | source)
XLA Modules:
  0.0 43.5 jit_solution(18235167569847706998)
XLA Ops:
  0.0 42.2 %shard_map.109 = bf16[32,160]{1,0:T(8,128)(2,1)} custom-call(bf16[128,3200]{1,0:T(8,128)(2,1)} %tk_h.1, bf16[128,640]{1,0:T(8,128)(2,1)} %tg_h.1, s32[1,128]{1,0:T(1,128)} %bitcast.9, bf16[3200,1024]{1,0:T(8,128)(2,1)} %kw_h.1, bf16[640,1024]{1,0:T(8,128)(2,1)} %gw_h.1, f32[1,1024]{1,0:T(1,128)} %bitcast.6, f32[1,1024]{1,0:T(1,128)} %bitcast.7, ...), custom_call_target="tpu_custom_call" | custom-call | flops 2000000000 | bytes 14000000 | tf_op jit(solution)/shard_map/pallas_call | solution.py:276
  42.2 1.3 %copy.13 = bf16[32,160]{1,0:T(8,128)(2,1)} copy(bf16[32,160]{1,0:T(8,128)(2,1)} %shard_map.109) | data formatting | bytes 20480

commit v3 on v2

--- a/solution.py
+++ b/solution.py
@@ -51,8 +51,13 @@
             src_ref=src, dst_ref=dst, send_sem=s, recv_sem=r, device_id=dev, device_id_type=MESH
         ).start()
 
-    def await_bytes(buf, sem):
-        pltpu.make_async_copy(buf, buf, sem).wait()
+    waits = {}
+
+    def expect(name, buf, sem):
+        waits[name] = pltpu.make_async_copy(buf, buf, sem).wait
+
+    def settle(name):
+        waits.pop(name)()
 
     core_rows = pl.ds(pl.multiple_of(c * HALF, HALF), HALF)
     loads = dict(
@@ -64,17 +69,21 @@
 
     def load(name):
         src, dst = loads[name]
-        return pltpu.make_async_copy(src, dst, lsem.at[number[name]])
+        copy = pltpu.make_async_copy(src, dst, lsem.at[number[name]])
+        copy.start()
+        waits[name] = copy.wait
 
     def load_kw(ch):
-        return pltpu.make_async_copy(kw_h.at[:, pl.ds(ch * CH, CH)], kw.at[ch], kwsem.at[ch])
+        copy = pltpu.make_async_copy(kw_h.at[:, pl.ds(ch * CH, CH)], kw.at[ch], kwsem.at[ch])
+        copy.start()
+        waits["kw", ch] = copy.wait
 
     for name in ("tk", "bank", "lids", "ids", "tg", "gw"):
-        load(name).start()
+        load(name)
     for ch in range(NCH):
-        load_kw(ch).start()
+        load_kw(ch)
     for name in ("bias", "gate", "dw", "go"):
-        load(name).start()
+        load(name)
 
     barrier = pltpu.get_barrier_semaphore()
     beside = [lax.rem(d + 1, 2 * NCHIP), lax.rem(d + 2 * NCHIP - 1, 2 * NCHIP)]
@@ -82,24 +91,24 @@
     greet = [sibling] + [(e, m) for e in beside]
     greet += [zdev(k) for k in range(1, NZ)]
     greet += [(chip(k) * 2 + c, m) for k in range(1, NCHIP)]
-    greet += [(4 * lax.rem(m + NZ // 2, NZ) + s, lax.div(d, 4)) for s in range(4)]
     for dev in greet:
         pl.semaphore_signal(barrier, inc=1, device_id=dev, device_id_type=MESH)
 
-    load("lids").wait()
+    settle("lids")
     ids_row = lids[...].astype(F32)
     pick_t = (
         lax.broadcasted_iota(jnp.int32, (BANK, ROWS), 0).astype(F32) == ids_row
     ).astype(F32).astype(BF16)
-    load("tk").wait()
-    load("bank").wait()
+    settle("tk")
+    settle("bank")
     bank_scores = lax.dot_general(tk[...], bank[...], NT, preferred_element_type=F32).astype(BF16)
     pbuf[NCH] = jnp.dot(bank_scores, pick_t, preferred_element_type=F32).astype(BF16)
-    load("tg").wait()
-    load("gw").wait()
 
     def partial_sum(ch):
-        load_kw(ch).wait()
+        if ch == 0:
+            settle("tg")
+            settle("gw")
+        settle(("kw", ch))
         value = jnp.dot(tk[...], kw[ch], preferred_element_type=F32)
         value = value + jnp.dot(
             tg[...], gw[:, ch * CH:(ch + 1) * CH], preferred_element_type=F32
@@ -107,23 +116,78 @@
         pbuf[ch] = value.astype(BF16)
 
     def send_partial(ch):
-        for k in range(1, NZ):
+        for k in (4, 3, 5, 2, 6, 1, 7):
             to = lax.rem(m + k, NZ)
             rows = pl.ds(pl.multiple_of(to * TB, TB), TB)
             remote(pbuf.at[ch, rows], rz.at[ch, k - 1], rz_s.at[ch], rz_r.at[ch], (d, to))
-
+        expect(("rz", ch), rz.at[ch], rz_r.at[ch])
+        expect(("rz sent", ch), rz.at[ch], rz_s.at[ch])
+
+    settle("ids")
+    pl.semaphore_wait(barrier, len(greet))
+    send_partial(NCH)
     partial_sum(0)
-    load("ids").wait()
-    pl.semaphore_wait(barrier, len(greet))
     send_partial(0)
-    send_partial(NCH)
     for i, e in enumerate(beside):
         remote(ids, near.at[i], i_s.at[i], i_r.at[i], (e, m))
+        expect(("near", i), near.at[i], i_r.at[i])
+        expect(("near sent", i), near.at[i], i_s.at[i])
     for ch in range(1, NCH):
         partial_sum(ch)
         send_partial(ch)
 
-    load("dw").wait()
+    own_ids = ids[...].astype(F32)
+    wanted = lax.broadcasted_iota(jnp.int32, (TB, TOK), 1) == (
+        lax.broadcasted_iota(jnp.int32, (TB, TOK), 0) + m * TB
+    )
+    ids_here = jnp.sum(jnp.where(wanted, jnp.broadcast_to(own_ids, (TB, TOK)), 0.0), axis=1, keepdims=True)
+    count = jnp.sum((ids_here == own_ids).astype(F32), axis=1, keepdims=True)
+    for i in range(2):
+        settle(("near", i))
+        count = count + jnp.sum((ids_here == near[i].astype(F32)).astype(F32), axis=1, keepdims=True)
+
+    settle("bias")
+    settle("gate")
+    mine = pl.ds(pl.multiple_of(m * TB, TB), TB)
+
+    def summed(ch):
+        settle(("rz", ch))
+        value = pbuf[ch, mine].astype(F32)
+        for k in range(NZ - 1):
+            value = value + rz[ch, k].astype(F32)
+        return value
+
+    gated = jnp.zeros((TB, 1), F32)
+    for ch in range(NCH):
+        cut = slice(ch * CH, (ch + 1) * CH)
+        hidden = jnp.maximum(summed(ch) + bias[:, cut], 0.0).astype(BF16)
+        hid[:, cut] = hidden
+        gated = gated + jnp.sum(hidden.astype(F32) * gate[:, cut], axis=1, keepdims=True)
+    weight = 2.0 / ((1.0 + jnp.exp(-gated)) * count)
+    sw = (summed(NCH) * weight).astype(BF16)
+    swt[mine] = sw
+
+    def half(core):
+        return pl.ds(pl.multiple_of(core * HALF, HALF), HALF)
+
+    uh_tx[...] = lax.dot_general(sw, hid[:, half(1 - c)], TN, preferred_element_type=F32).astype(BF16)
+    remote(uh_tx, uh_rx, c_s.at[0], c_r.at[0], sibling)
+    expect("uh_rx", uh_rx, c_r.at[0])
+    expect("uh_tx sent", uh_rx, c_s.at[0])
+    for k in range(1, NZ):
+        remote(swt.at[mine], swt.at[mine], a_s.at[0], a_r.at[0], zdev(k))
+    expect("swt", swt.at[pl.ds(0, TOK - TB)], a_r.at[0])
+    expect("swt sent", swt.at[pl.ds(0, TOK - TB)], a_s.at[0])
+    own = lax.dot_general(sw, hid[:, half(c)], TN, preferred_element_type=F32)
+    settle("uh_rx")
+    uh_sum[...] = (own + uh_rx[...].astype(F32)).astype(BF16)
+    for k in range(1, NCHIP):
+        to = chip(k)
+        remote(uh_sum.at[rows_of(to)], uh_rs.at[k - 1], x_s.at[0], x_r.at[0], (to * 2 + c, m))
+    expect("uh_rs", uh_rs, x_r.at[0])
+    expect("uh_rs sent", uh_rs, x_s.at[0])
+
+    settle("dw")
     square = lax.broadcasted_iota(jnp.int32, (ROWS, ROWS), 0) == lax.broadcasted_iota(
         jnp.int32, (ROWS, ROWS), 1
     )
@@ -138,83 +202,46 @@
         remote(
             bbuf.at[pl.ds(pl.multiple_of(to * OB, OB), OB)], br.at[k - 1], b_s.at[0], b_r.at[0], (d, to)
         )
-
-    own_ids = ids[...].astype(F32)
-    wanted = lax.broadcasted_iota(jnp.int32, (TB, TOK), 1) == (
-        lax.broadcasted_iota(jnp.int32, (TB, TOK), 0) + m * TB
-    )
-    ids_here = jnp.sum(jnp.where(wanted, jnp.broadcast_to(own_ids, (TB, TOK)), 0.0), axis=1, keepdims=True)
-    count = jnp.sum((ids_here == own_ids).astype(F32), axis=1, keepdims=True)
-    for i in range(2):
-        pltpu.make_async_copy(ids, near.at[i], i_r.at[i]).wait()
-        count = count + jnp.sum((ids_here == near[i].astype(F32)).astype(F32), axis=1, keepdims=True)
-
-    load("bias").wait()
-    load("gate").wait()
-    mine = pl.ds(pl.multiple_of(m * TB, TB), TB)
-
-    def summed(ch):
-        await_bytes(rz.at[ch], rz_r.at[ch])
-        value = pbuf[ch, mine].astype(F32)
-        for k in range(NZ - 1):
-            value = value + rz[ch, k].astype(F32)
-        return value
-
-    gated = jnp.zeros((TB, 1), F32)
-    for ch in range(NCH):
-        cut = slice(ch * CH, (ch + 1) * CH)
-        hidden = jnp.maximum(summed(ch) + bias[:, cut], 0.0).astype(BF16)
-        hid[:, cut] = hidden
-        gated = gated + jnp.sum(hidden.astype(F32) * gate[:, cut], axis=1, keepdims=True)
-    weight = 2.0 / ((1.0 + jnp.exp(-gated)) * count)
-    sw = (summed(NCH) * weight).astype(BF16)
-    swt[mine] = sw
-    for k in range(1, NZ):
-        remote(swt.at[mine], swt.at[mine], a_s.at[0], a_r.at[0], zdev(k))
-
-    def half(core):
-        return pl.ds(pl.multiple_of(core * HALF, HALF), HALF)
-
-    uh_tx[...] = lax.dot_general(sw, hid[:, half(1 - c)], TN, preferred_element_type=F32).astype(BF16)
-    remote(uh_tx, uh_rx, c_s.at[0], c_r.at[0], sibling)
-    own = lax.dot_general(sw, hid[:, half(c)], TN, preferred_element_type=F32)
-    await_bytes(uh_rx, c_r.at[0])
-    uh_sum[...] = (own + uh_rx[...].astype(F32)).astype(BF16)
-    for k in range(1, NCHIP):
-        to = chip(k)
-        remote(uh_sum.at[rows_of(to)], uh_rs.at[k - 1], x_s.at[0], x_r.at[0], (to * 2 + c, m))
+    expect("br", br, b_r.at[0])
+    expect("br sent", br, b_s.at[0])
 
     def window(core):
         return pl.ds(pl.multiple_of(core * 256, 256), WIDE)
 
-    await_bytes(swt.at[pl.ds(0, TOK - TB)], a_r.at[0])
+    settle("swt")
     scores = swt[...]
     ug_tx[...] = lax.dot_general(scores, tg[:, window(1 - c)], TN, preferred_element_type=F32).astype(BF16)
     remote(ug_tx, ug_rx, c_s.at[1], c_r.at[1], sibling)
+    expect("ug_rx", ug_rx, c_r.at[1])
+    expect("ug_tx sent", ug_rx, c_s.at[1])
     own = lax.dot_general(scores, tg[:, window(c)], TN, preferred_element_type=F32)
-    await_bytes(ug_rx, c_r.at[1])
+    settle("ug_rx")
     ug_sum[...] = (own + ug_rx[...].astype(F32)).astype(BF16)
     for k in range(1, NCHIP):
         to = chip(k)
         remote(ug_sum.at[rows_of(to)], ug_rs.at[k - 1], x_s.at[1], x_r.at[1], (to * 2 + c, m))
-
-    await_bytes(uh_rs, x_r.at[0])
+    expect("ug_rs", ug_rs, x_r.at[1])
+    expect("ug_rs sent", ug_rs, x_s.at[1])
+
+    settle("uh_rs")
     value = uh_sum[rows_of(q)].astype(F32)
     for k in range(NCHIP - 1):
         value = value + uh_rs[k].astype(F32)
     uz_tx[...] = value.astype(BF16)
     for k in range(1, NZ):
         remote(uz_tx, uz.at[k - 1], z_s.at[0], z_r.at[0], zdev(k))
-
-    await_bytes(ug_rs, x_r.at[1])
+    expect("uz", uz, z_r.at[0])
+    expect("uz sent", uz, z_s.at[0])
+
+    settle("ug_rs")
     grads_part = ug_sum[rows_of(q)].astype(F32)
     for k in range(NCHIP - 1):
         grads_part = grads_part + ug_rs[k].astype(F32)
     lane = lax.broadcasted_iota(jnp.int32, (RB, WIDE), 1)
     grads_part = jnp.where(lane >= c * 128, grads_part, 0.0)
 
-    load("go").wait()
-    await_bytes(uz, z_r.at[0])
+    settle("go")
+    settle("uz")
     for k in range(NZ - 1):
         value = value + uz[k].astype(F32)
     mm[...] = jnp.dot(value.astype(BF16), go[...], preferred_element_type=F32)
@@ -223,30 +250,22 @@
     slot = lax.rem(d, 4)
     for j in range(4):
         remote(ftx.at[:, pl.ds(128 * j, 256)], frx.at[slot], f_s.at[0], f_r.at[0], (4 * m + j, target))
-
-    await_bytes(br, b_r.at[0])
+    expect("frx", frx, f_r.at[0])
+    expect("frx sent", frx, f_s.at[0])
+
+    settle("br")
     base = bbuf[pl.ds(pl.multiple_of(m * OB, OB), OB)].astype(F32)
     for k in range(NZ - 1):
         base = base + br[k].astype(F32)
-    await_bytes(frx, f_r.at[0])
+    settle("frx")
     spread = jnp.concatenate(
         [frx[0].astype(F32) + frx[1].astype(F32), frx[2].astype(F32) + frx[3].astype(F32)], axis=0
     )
     spread = pltpu.roll(spread, lax.rem(256 - 32 * slot, 256), 1)
     out_ref[...] = (base + SCALE * spread[:, :COLS]).astype(BF16)
 
-    for ch in range(NCH + 1):
-        await_bytes(rz.at[ch], rz_s.at[ch])
-    await_bytes(br, b_s.at[0])
-    for i in range(2):
-        pltpu.make_async_copy(ids, near.at[i], i_s.at[i]).wait()
-    await_bytes(swt.at[pl.ds(0, TOK - TB)], a_s.at[0])
-    await_bytes(uh_rx, c_s.at[0])
-    await_bytes(ug_rx, c_s.at[1])
-    await_bytes(uh_rs, x_s.at[0])
-    await_bytes(ug_rs, x_s.at[1])
-    await_bytes(uz, z_s.at[0])
-    await_bytes(frx, f_s.at[0])
+    for name in list(waits):
+        settle(name)
 
 
 def local(
@@ -275,7 +294,7 @@
     any_spec = pl.BlockSpec(memory_space=pl.ANY)
     return pl.pallas_call(
         kernel,
-        out_shape=jax.ShapeDtypeStruct((OB, COLS), BF16),
+        out_shape=pltpu.VMEM((OB, COLS), BF16),
         in_specs=[any_spec] * 11,
         out_specs=pl.BlockSpec(memory_space=pltpu.VMEM),
         scratch_shapes=scratch,

time: 43.7 us -> 39.3 us (0.90)
  Pallas kernels: 42.2 us -> 38.4 us
  local copies, waits for them, and re-layouts: 1.32 us -> 0.61 us
    pallas_call x1, Pallas kernels: 42.2 us -> 38.4 us  [local(): pl.pallas_call(kernel, out_shape=pltpu.VMEM((OB, COLS), BF16), in_specs=[...]
    unnamed x1, local copies, waits for them, and re-layouts: 1.32 us -> 0.61 us
where the time goes in v3:
time: 39.3 us; the launch traced here: 39.1 us
  Pallas kernels  38.4 us (98%)
  local copies, waits for them, and re-layouts  0.61 us (2%)
    pallas_call x1, Pallas kernels, local(): pl.pallas_call(kernel, out_shape=pltpu.VMEM((OB, COLS), BF16), in_specs=[...  38.4 us

profile of v3, /device:TPU:7, one launch (start us, length us, event | category | flops | bytes accessed | tf_op | source)
XLA Modules:
  0.0 39.1 jit_solution(8312484411215563174)
XLA Ops:
  0.0 38.4 %shard_map.109 = bf16[32,160]{1,0:T(8,128)(2,1)S(1)} custom-call(bf16[128,3200]{1,0:T(8,128)(2,1)} %tk_h.1, bf16[128,640]{1,0:T(8,128)(2,1)} %tg_h.1, s32[1,128]{1,0:T(1,128)} %bitcast.9, bf16[3200,1024]{1,0:T(8,128)(2,1)} %kw_h.1, bf16[640,1024]{1,0:T(8,128)(2,1)} %gw_h.1, f32[1,1024]{1,0:T(1,128)} %bitcast.6, f32[1,1024]{1,0:T(1,128)} %bitcast.7, ...), custom_call_target="tpu_custom_call" | custom-call | flops 2000000000 | bytes 14000000 | tf_op jit(solution)/shard_map/pallas_call | solution.py:295
  38.5 0.6 %copy.13 = bf16[32,160]{1,0:T(8,128)(2,1)} copy(bf16[32,160]{1,0:T(8,128)(2,1)S(1)} %shard_map.109) | data formatting | bytes 20480

commit v4 on v3

v4 whole, which is shorter than its diff:
```python
import jax
import jax.numpy as jnp
from jax import lax
from jax.experimental import pallas as pl
from jax.experimental.pallas import tpu as pltpu
from jax.sharding import PartitionSpec as P

MESH = pl.DeviceIdType.MESH
F32, BF16 = jnp.float32, jnp.bfloat16
NZ, NX, NY, NCHIP = 8, 4, 4, 16
TOK, KEYS, GRADS, HID, ROWS, BANK, COLS = 128, 3200, 640, 1024, 256, 320, 160
TB = TOK // NZ
RB = ROWS // NCHIP
HALF = HID // 2
WIDE = 384
CH = 256
NCH = HID // CH
OB = ROWS // NZ
SCALE = 4.0 / 10240.0

FAR = sorted(range(1, NCHIP), key=lambda k: -(min(k // NX, NY - k // NX) + min(k % NX, NX - k % NX)))

TN = (((0,), (0,)), ((), ()))
NT = (((1,), (1,)), ((), ()))


def kernel(
    tk_h, tg_h, ids_h, kw_h, gw_h, bias_h, gate_h, go_h, dw_h, bank_h, lids_h,
    out_ref,
    tk, tg, ids, kw, gw, bias, gate, go, dw, bank, lids,
    near, factor, pbuf, rz, bbuf, br, hid, sw2, hid2, swx, uh_sum, uh_rs, ug_sum, ug_rs,
    uz_tx, uz, ftx, frx, gtx, grx,
    lsem, kwsem, rz_s, rz_r, b_s, b_r, i_s, i_r, a_s, a_r, c_s, c_r, x_s, x_r, z_s, z_r, f_s, f_r, g_s, g_r,
):
    d, m = lax.axis_index("dp"), lax.axis_index("mp")
    c = lax.rem(d, 2)
    q = lax.div(d, 2)
    y, x = lax.div(q, NX), lax.rem(q, NX)
    sibling = (d + 1 - 2 * c, m)

    def zdev(k):
        return (d, lax.rem(m + k, NZ))

    def chip(k):
        ky, kx = divmod(k, NX)
        return lax.rem(y + ky, NY) * NX + lax.rem(x + kx, NX)

    def rows_of(chip_index):
        block = lax.rem(chip_index, 2) * NZ + lax.rem(lax.div(chip_index, 2) + NZ // 2, NZ)
        return pl.ds(pl.multiple_of(block * RB, RB), RB)

    def place(chip_index):
        dx = lax.rem(lax.rem(chip_index, NX) - 2 * lax.rem(m, 2) + NX, NX)
        dy = lax.rem(lax.div(chip_index, NX) - lax.div(m, 2) + NY, NY)
        side, far = lax.rem(lax.div(dx + 1, 2), 2), lax.div(dx, 2)
        step = (1 - far) * (lax.rem(dy + 2, 4) + 2) + far * lax.rem(dy + 6, 8)
        return side, lax.rem(m + step, NZ)

    def piece(chip_index):
        side, block = place(chip_index)
        return pl.ds(pl.multiple_of(block * RB, RB), RB), pl.ds(pl.multiple_of(side * 256, 256), WIDE)

    def remote(src, dst, s, r, dev):
        pltpu.make_async_remote_copy(
            src_ref=src, dst_ref=dst, send_sem=s, recv_sem=r, device_id=dev, device_id_type=MESH
        ).start()

    waits = {}

    def expect(name, buf, sem):
        waits[name] = pltpu.make_async_copy(buf, buf, sem).wait

    def settle(name):
        waits.pop(name)()

    core_tokens = pl.ds(pl.multiple_of(c * TOK, TOK), TOK)
    core_rows16 = pl.ds(pl.multiple_of(c * TB, TB), TB)
    core_rows = pl.ds(pl.multiple_of(c * HALF, HALF), HALF)
    loads = dict(
        tk=(tk_h, tk), bank=(bank_h, bank), lids=(lids_h, lids), tg=(tg_h, tg.at[core_tokens]),
        ids=(ids_h, ids), bias=(bias_h, bias), gate=(gate_h, gate),
        dw=(dw_h, dw), go=(go_h.at[core_rows], go),
    )
    number = {name: i for i, name in enumerate(loads)}

    def load(name):
        src, dst = loads[name]
        copy = pltpu.make_async_copy(src, dst, lsem.at[number[name]])
        copy.start()
        waits[name] = copy.wait

    def load_kw(ch):
        copy = pltpu.make_async_copy(kw_h.at[:, pl.ds(ch * CH, CH)], kw.at[ch], kwsem.at[ch])
        copy.start()
        waits["kw", ch] = copy.wait
        copy = pltpu.make_async_copy(gw_h.at[:, pl.ds(ch * CH, CH)], gw.at[ch], kwsem.at[NCH + ch])
        copy.start()
        waits["gw", ch] = copy.wait

    for name in ("lids", "tk", "bank", "tg", "ids", "bias", "gate"):
        load(name)

    barrier = pltpu.get_barrier_semaphore()
    beside = [lax.rem(d + 1, 2 * NCHIP), lax.rem(d + 2 * NCHIP - 1, 2 * NCHIP)]
    target = lax.rem(lax.div(d, 4) + NZ // 2, NZ)
    greet = [sibling] + [(e, m) for e in beside]
    greet += [zdev(k) for k in range(1, NZ)]
    greet += [(chip(k) * 2 + c, m) for k in range(1, NCHIP)]
    for dev in greet:
        pl.semaphore_signal(barrier, inc=1, device_id=dev, device_id_type=MESH)

    settle("lids")
    ids_row = lids[...].astype(F32)
    rows0 = lax.broadcasted_iota(jnp.int32, (ROWS, ROWS), 0)
    rows1 = lax.broadcasted_iota(jnp.int32, (ROWS, ROWS), 1)
    ids_col = jnp.sum(
        jnp.where(rows0 == rows1, jnp.broadcast_to(ids_row, (ROWS, ROWS)), 0.0), axis=1, keepdims=True
    )
    ordered = 32 * ((rows1 >> 4) & 7) + 16 * (rows1 >> 7) + (rows1 & 15)
    ids_ordered = jnp.sum(
        jnp.where(rows0 == ordered, jnp.broadcast_to(ids_col, (ROWS, ROWS)), 0.0), axis=0, keepdims=True
    )
    pick_t = (
        lax.broadcasted_iota(jnp.int32, (BANK, ROWS), 0).astype(F32) == ids_ordered
    ).astype(F32).astype(BF16)
    load_kw(0)
    settle("tk")
    settle("tg")

    def bank_part():
        settle("bank")
        bank_scores = lax.dot_general(tk[...], bank[...], NT, preferred_element_type=F32).astype(BF16)
        pbuf[NCH] = jnp.dot(bank_scores, pick_t, preferred_element_type=F32).astype(BF16)

    bank_part()
    load_kw(1)

    def partial_sum(ch):
        settle(("kw", ch))
        settle(("gw", ch))
        if ch + 2 < NCH:
            load_kw(ch + 2)
        elif ch + 2 == NCH:
            load("dw")
        else:
            load("go")
        value = jnp.dot(tk[...], kw[ch], preferred_element_type=F32)
        value = value + jnp.dot(
            tg[core_tokens], gw[ch], preferred_element_type=F32
        )
        pbuf[ch] = value.astype(BF16)

    def send_partial(first, many):
        for k in (4, 3, 5, 2, 6, 1, 7):
            to = lax.rem(m + k, NZ)
            rows = pl.ds(pl.multiple_of(to * TB, TB), TB)
            remote(
                pbuf.at[pl.ds(first, many), rows], rz.at[pl.ds(first, many), k - 1],
                rz_s.at[first], rz_r.at[first], (d, to),
            )
        expect(("rz", first), rz.at[pl.ds(first, many)], rz_r.at[first])
        expect(("rz sent", first), rz.at[pl.ds(first, many)], rz_s.at[first])

    settle("ids")
    pl.semaphore_wait(barrier, len(greet))
    send_partial(NCH, 1)
    partial_sum(0)
    send_partial(0, 1)
    remote(tg.at[core_tokens], tg.at[core_tokens], c_s.at[2], c_r.at[2], sibling)
    expect("tg other", tg.at[core_tokens], c_r.at[2])
    expect("tg sent", tg.at[core_tokens], c_s.at[2])
    for i, e in enumerate(beside):
        remote(ids, near.at[i], i_s.at[i], i_r.at[i], (e, m))
        expect(("near", i), near.at[i], i_r.at[i])
        expect(("near sent", i), near.at[i], i_s.at[i])
    for ch in range(1, NCH):
        partial_sum(ch)
        if ch == NCH - 1:
            send_partial(1, 3)

    own_ids = ids[...].astype(F32)
    wanted = lax.broadcasted_iota(jnp.int32, (TB, TOK), 1) == (
        lax.broadcasted_iota(jnp.int32, (TB, TOK), 0) + m * TB
    )
    ids_here = jnp.sum(jnp.where(wanted, jnp.broadcast_to(own_ids, (TB, TOK)), 0.0), axis=1, keepdims=True)
    count = jnp.sum((ids_here == own_ids).astype(F32), axis=1, keepdims=True)
    for i in range(2):
        settle(("near", i))
        count = count + jnp.sum((ids_here == near[i].astype(F32)).astype(F32), axis=1, keepdims=True)

    factor[...] = jnp.broadcast_to(2.0 / count, (TB, ROWS))
    settle("bias")
    settle("gate")
    mine = pl.ds(pl.multiple_of(m * TB, TB), TB)

    def summed(ch):
        if ("rz", ch) in waits:
            settle(("rz", ch))
        value = pbuf[ch, mine].astype(F32)
        for k in range(NZ - 1):
            value = value + rz[ch, k].astype(F32)
        return value

    gated = jnp.zeros((TB, CH), F32)
    for ch in range(NCH):
        cut = slice(ch * CH, (ch + 1) * CH)
        hidden = jnp.maximum(summed(ch) + bias[:, cut], 0.0).astype(BF16)
        hid[:, cut] = hidden
        gated = gated + hidden.astype(F32) * gate[:, cut]
    weight = jax.nn.sigmoid(jnp.sum(gated, axis=1, keepdims=True)) * factor[...]
    def half(core):
        return pl.ds(pl.multiple_of(core * HALF, HALF), HALF)

    remote(hid.at[:, half(1 - c)], hid2.at[core_rows16], c_s.at[1], c_r.at[1], sibling)
    expect("hid2", hid2.at[core_rows16], c_r.at[1])
    expect("hid2 sent", hid2.at[core_rows16], c_s.at[1])
    hid2[core_rows16] = hid[:, half(c)]
    sw2[core_rows16] = (summed(NCH) * weight).astype(BF16)
    remote(sw2.at[core_rows16], sw2.at[core_rows16], c_s.at[0], c_r.at[0], sibling)
    expect("sw2", sw2.at[core_rows16], c_r.at[0])
    expect("sw2 sent", sw2.at[core_rows16], c_s.at[0])

    def lanes(core):
        return pl.ds(pl.multiple_of(core * 128, 128), 128)

    my_tokens = pl.ds(pl.multiple_of(c * TOK + m * TB, TB), TB)

    def send_scores(core, k):
        remote(
            sw2.at[core_rows16, lanes(core)], swx.at[my_tokens], a_s.at[0], a_r.at[0],
            (q * 2 + core, lax.rem(m + k, NZ)),
        )

    settle("hid2")
    settle("sw2")
    for part in range(2):
        units = slice(part * CH, (part + 1) * CH)
        uh_sum[part] = lax.dot_general(sw2[...], hid2[:, units], TN, preferred_element_type=F32).astype(BF16)
        for k in FAR:
            to = chip(k)
            remote(
                uh_sum.at[part, rows_of(to)], uh_rs.at[part, k - 1], x_s.at[part], x_r.at[part], (to * 2 + c, m)
            )
        expect(("uh_rs", part), uh_rs.at[part], x_r.at[part])
        expect(("uh_rs sent", part), uh_rs.at[part], x_s.at[part])

    swx[my_tokens] = sw2[core_rows16, lanes(c)]
    for k in (4, 3, 5, 2, 6, 1, 7):
        for core in range(2):
            send_scores(core, k)
    send_scores(1 - c, 0)
    expect("swx", swx.at[pl.ds(0, 2 * TOK - TB)], a_r.at[0])
    expect("swx sent", swx.at[pl.ds(0, 2 * TOK - TB)], a_s.at[0])

    settle("dw")
    pick = (
        lax.broadcasted_iota(jnp.int32, (ROWS, BANK), 1).astype(F32) == ids_col
    ).astype(F32).astype(BF16)
    bank_down = lax.dot_general(bank[...], dw[...], NT, preferred_element_type=F32).astype(BF16)
    bbuf[...] = jnp.dot(pick, bank_down, preferred_element_type=F32).astype(BF16)
    for k in range(1, NZ):
        to = lax.rem(m + k, NZ)
        remote(
            bbuf.at[pl.ds(pl.multiple_of(to * OB, OB), OB)], br.at[k - 1], b_s.at[0], b_r.at[0], (d, to)
        )
    expect("br", br, b_r.at[0])
    expect("br sent", br, b_s.at[0])

    settle("tg other")
    settle("swx")
    ug_sum[...] = lax.dot_general(swx[...], tg[...], TN, preferred_element_type=F32).astype(BF16)
    for k in FAR:
        to = chip(k)
        remote(ug_sum.at[piece(to)], ug_rs.at[k - 1], x_s.at[2], x_r.at[2], (to * 2 + c, m))
    expect("ug_rs", ug_rs, x_r.at[2])
    expect("ug_rs sent", ug_rs, x_s.at[2])

    plane = []
    for part in range(2):
        settle(("uh_rs", part))
        value = uh_sum[part, rows_of(q)].astype(F32)
        for k in range(NCHIP - 1):
            value = value + uh_rs[part, k].astype(F32)
        plane.append(value)
        uz_tx[part] = value.astype(BF16)
        for k in (4, 3, 5, 2, 6, 1, 7):
            remote(uz_tx.at[part], uz.at[part, k - 1], z_s.at[part], z_r.at[part], zdev(k))
        expect(("uz", part), uz.at[part], z_r.at[part])
        expect(("uz sent", part), uz.at[part], z_s.at[part])

    settle("ug_rs")
    grads_part = ug_sum[piece(q)].astype(F32)
    for k in range(NCHIP - 1):
        grads_part = grads_part + ug_rs[k].astype(F32)
    gtx[...] = grads_part.astype(BF16)
    side, block = place(q)
    for j in range(2):
        remote(
            gtx.at[:, pl.ds(128 * j, 256)], grx.at[c], g_s.at[0], g_r.at[0], (4 * m + 2 * side + j, block)
        )
    expect("grx", grx, g_r.at[0])
    expect("grx sent", grx, g_s.at[0])

    settle("go")
    product = jnp.zeros((RB, GRADS), F32)
    for part in range(2):
        settle(("uz", part))
        value = plane[part]
        for k in range(NZ - 1):
            value = value + uz[part, k].astype(F32)
        product = product + jnp.dot(
            value.astype(BF16), go[part * CH:(part + 1) * CH], preferred_element_type=F32
        )
    ftx[...] = product.astype(BF16)
    slot = lax.rem(d, 4)
    for j in range(4):
        remote(ftx.at[:, pl.ds(128 * j, 256)], frx.at[slot], f_s.at[0], f_r.at[0], (4 * m + j, target))
    expect("frx", frx, f_r.at[0])
    expect("frx sent", frx, f_s.at[0])

    settle("br")
    base = bbuf[pl.ds(pl.multiple_of(m * OB, OB), OB)].astype(F32)
    for k in range(NZ - 1):
        base = base + br[k].astype(F32)
    settle("grx")
    settle("frx")
    spread = jnp.concatenate(
        [
            frx[0].astype(F32) + frx[1].astype(F32) + grx[0].astype(F32),
            frx[2].astype(F32) + frx[3].astype(F32) + grx[1].astype(F32),
        ],
        axis=0,
    )
    spread = pltpu.roll(spread, lax.rem(256 - 32 * slot, 256), 1)
    out_ref[...] = (base + SCALE * spread[:, :COLS]).astype(BF16)

    for name in list(waits):
        settle(name)


def local(
    token_keys, token_grads, prompt_ids, key_weight, grad_weight, hidden_bias, gate_vector, grad_output,
    down_weight, locality_bank, locality_ids,
):
    vm = pltpu.VMEM
    dma = pltpu.SemaphoreType.DMA
    scratch = [
        vm((TOK, KEYS), BF16), vm((2 * TOK, GRADS), BF16), vm((1, TOK), jnp.int32),
        vm((NCH, KEYS, CH), BF16), vm((NCH, GRADS, CH), BF16), vm((1, HID), F32), vm((1, HID), F32),
        vm((HALF, GRADS), BF16), vm((COLS, KEYS), BF16), vm((BANK, KEYS), BF16), vm((1, ROWS), jnp.int32),
        vm((2, 1, TOK), jnp.int32), vm((TB, ROWS), F32),
        vm((NCH + 1, TOK, CH), BF16), vm((NCH + 1, NZ - 1, TB, CH), BF16),
        vm((ROWS, COLS), BF16), vm((NZ - 1, OB, COLS), BF16),
        vm((TB, HID), BF16), vm((2 * TB, ROWS), BF16), vm((2 * TB, HALF), BF16), vm((2 * TOK, 128), BF16),
        vm((2, ROWS, CH), BF16), vm((2, NCHIP - 1, RB, CH), BF16),
        vm((ROWS // 2, GRADS), BF16), vm((NCHIP - 1, RB, WIDE), BF16),
        vm((2, RB, CH), BF16), vm((2, NZ - 1, RB, CH), BF16),
        vm((RB, GRADS), BF16), vm((4, RB, 256), BF16), vm((RB, WIDE), BF16), vm((2, RB, 256), BF16),
        dma((10,)), dma((2 * NCH,)), dma((NCH + 1,)), dma((NCH + 1,)), dma((1,)), dma((1,)), dma((2,)), dma((2,)),
        dma((1,)), dma((1,)), dma((3,)), dma((3,)), dma((3,)), dma((3,)), dma((2,)), dma((2,)), dma((1,)), dma((1,)),
        dma((1,)), dma((1,)),
    ]
    any_spec = pl.BlockSpec(memory_space=pl.ANY)
    return pl.pallas_call(
        kernel,
        out_shape=pltpu.VMEM((OB, COLS), BF16),
        in_specs=[any_spec] * 11,
        out_specs=pl.BlockSpec(memory_space=pltpu.VMEM),
        scratch_shapes=scratch,
        compiler_params=pltpu.CompilerParams(
            collective_id=0, has_side_effects=True, vmem_limit_bytes=60 * 1024 * 1024
        ),
        cost_estimate=pl.CostEstimate(flops=2_000_000_000, bytes_accessed=14_000_000, transcendentals=16),
    )(
        token_keys, token_grads, prompt_ids.reshape(1, TOK), key_weight, grad_weight,
        hidden_bias.reshape(1, HID), gate_vector.reshape(1, HID), grad_output, down_weight.T, locality_bank,
        locality_ids.reshape(1, ROWS),
    )


def solution(mesh):
    placed = (
        P("dp", "mp"), P("dp", "mp"), P("dp"), P("mp", None), P("mp", None), P(), P(), P(None, "mp"),
        P("mp", "dp"), P(None, "mp"), P(),
    )
    return jax.shard_map(
        local, mesh=mesh, in_specs=placed, out_specs=P("mp", "dp"), check_vma=False
    )
```

time: 39.3 us -> 38.6 us (0.982); the launches traced: 39.1 us -> 37.9 us
  Pallas kernels: 38.4 us -> 37.3 us
    pallas_call x1, Pallas kernels: 38.4 us -> 37.3 us  [local(): pl.pallas_call(kernel, out_shape=pltpu.VMEM((OB, COLS), BF16), in_specs=[...]
where the time goes in v4:
time: 38.6 us; the launch traced here: 37.9 us
  Pallas kernels  37.3 us (97%)
  local copies, waits for them, and re-layouts  0.61 us (2%)
    pallas_call x1, Pallas kernels, local(): pl.pallas_call(kernel, out_shape=pltpu.VMEM((OB, COLS), BF16), in_specs=[...  37.3 us

profile of v4, /device:TPU:7, one launch (start us, length us, event | category | flops | bytes accessed | tf_op | source)
XLA Modules:
  0.0 37.9 jit_solution(15193372675777051482)
XLA Ops:
  0.0 37.3 %shard_map.109 = bf16[32,160]{1,0:T(8,128)(2,1)S(1)} custom-call(bf16[128,3200]{1,0:T(8,128)(2,1)} %tk_h.1, bf16[128,640]{1,0:T(8,128)(2,1)} %tg_h.1, s32[1,128]{1,0:T(1,128)} %bitcast.9, bf16[3200,1024]{1,0:T(8,128)(2,1)} %kw_h.1, bf16[640,1024]{1,0:T(8,128)(2,1)} %gw_h.1, f32[1,1024]{1,0:T(1,128)} %bitcast.6, f32[1,1024]{1,0:T(1,128)} %bitcast.7, ...), custom_call_target="tpu_custom_call" | custom-call | flops 2000000000 | bytes 14000000 | tf_op jit(solution)/shard_map/pallas_call | solution.py:364
  37.3 0.6 %copy.13 = bf16[32,160]{1,0:T(8,128)(2,1)} copy(bf16[32,160]{1,0:T(8,128)(2,1)S(1)} %shard_map.109) | data formatting | bytes 20480

commit v5 on v4

--- a/solution.py
+++ b/solution.py
@@ -65,6 +65,15 @@
             src_ref=src, dst_ref=dst, send_sem=s, recv_sem=r, device_id=dev, device_id_type=MESH
         ).start()
 
+    barrier = pltpu.get_barrier_semaphore()
+    beside = [lax.rem(d + 1, 2 * NCHIP), lax.rem(d + 2 * NCHIP - 1, 2 * NCHIP)]
+    target = lax.rem(lax.div(d, 4) + NZ // 2, NZ)
+    greet = [zdev(k) for k in (4, 3, 5, 2, 6, 1, 7)]
+    greet += [(chip(k) * 2 + c, m) for k in FAR]
+    greet += [sibling] + [(e, m) for e in beside]
+    for dev in greet:
+        pl.semaphore_signal(barrier, inc=1, device_id=dev, device_id_type=MESH)
+
     waits = {}
 
     def expect(name, buf, sem):
@@ -99,15 +108,6 @@
 
     for name in ("lids", "tk", "bank", "tg", "ids", "bias", "gate"):
         load(name)
-
-    barrier = pltpu.get_barrier_semaphore()
-    beside = [lax.rem(d + 1, 2 * NCHIP), lax.rem(d + 2 * NCHIP - 1, 2 * NCHIP)]
-    target = lax.rem(lax.div(d, 4) + NZ // 2, NZ)
-    greet = [sibling] + [(e, m) for e in beside]
-    greet += [zdev(k) for k in range(1, NZ)]
-    greet += [(chip(k) * 2 + c, m) for k in range(1, NCHIP)]
-    for dev in greet:
-        pl.semaphore_signal(barrier, inc=1, device_id=dev, device_id_type=MESH)
 
     settle("lids")
     ids_row = lids[...].astype(F32)
@@ -178,6 +178,13 @@
         if ch == NCH - 1:
             send_partial(1, 3)
 
+    settle("dw")
+    pick = (
+        lax.broadcasted_iota(jnp.int32, (ROWS, BANK), 1).astype(F32) == ids_col
+    ).astype(F32).astype(BF16)
+    bank_down = lax.dot_general(bank[...], dw[...], NT, preferred_element_type=F32).astype(BF16)
+    bbuf[...] = jnp.dot(pick, bank_down, preferred_element_type=F32).astype(BF16)
+
     own_ids = ids[...].astype(F32)
     wanted = lax.broadcasted_iota(jnp.int32, (TB, TOK), 1) == (
         lax.broadcasted_iota(jnp.int32, (TB, TOK), 0) + m * TB
@@ -230,6 +237,14 @@
             sw2.at[core_rows16, lanes(core)], swx.at[my_tokens], a_s.at[0], a_r.at[0],
             (q * 2 + core, lax.rem(m + k, NZ)),
         )
+
+    swx[my_tokens] = sw2[core_rows16, lanes(c)]
+    for k in (4, 3, 5, 2, 6, 1, 7):
+        for core in range(2):
+            send_scores(core, k)
+    send_scores(1 - c, 0)
+    expect("swx", swx.at[pl.ds(0, 2 * TOK - TB)], a_r.at[0])
+    expect("swx sent", swx.at[pl.ds(0, 2 * TOK - TB)], a_s.at[0])
 
     settle("hid2")
     settle("sw2")
@@ -244,20 +259,6 @@
         expect(("uh_rs", part), uh_rs.at[part], x_r.at[part])
         expect(("uh_rs sent", part), uh_rs.at[part], x_s.at[part])
 
-    swx[my_tokens] = sw2[core_rows16, lanes(c)]
-    for k in (4, 3, 5, 2, 6, 1, 7):
-        for core in range(2):
-            send_scores(core, k)
-    send_scores(1 - c, 0)
-    expect("swx", swx.at[pl.ds(0, 2 * TOK - TB)], a_r.at[0])
-    expect("swx sent", swx.at[pl.ds(0, 2 * TOK - TB)], a_s.at[0])
-
-    settle("dw")
-    pick = (
-        lax.broadcasted_iota(jnp.int32, (ROWS, BANK), 1).astype(F32) == ids_col
-    ).astype(F32).astype(BF16)
-    bank_down = lax.dot_general(bank[...], dw[...], NT, preferred_element_type=F32).astype(BF16)
-    bbuf[...] = jnp.dot(pick, bank_down, preferred_element_type=F32).astype(BF16)
     for k in range(1, NZ):
         to = lax.rem(m + k, NZ)
         remote(
@@ -288,6 +289,23 @@
         expect(("uz", part), uz.at[part], z_r.at[part])
         expect(("uz sent", part), uz.at[part], z_s.at[part])
 
+    settle("go")
+    product = jnp.zeros((RB, GRADS), F32)
+    for part in range(2):
+        settle(("uz", part))
+        value = plane[part]
+        for k in range(NZ - 1):
+            value = value + uz[part, k].astype(F32)
+        product = product + jnp.dot(
+            value.astype(BF16), go[part * CH:(part + 1) * CH], preferred_element_type=F32
+        )
+    ftx[...] = product.astype(BF16)
+    slot = lax.rem(d, 4)
+    for j in range(4):
+        remote(ftx.at[:, pl.ds(128 * j, 256)], frx.at[slot], f_s.at[0], f_r.at[0], (4 * m + j, target))
+    expect("frx", frx, f_r.at[0])
+    expect("frx sent", frx, f_s.at[0])
+
     settle("ug_rs")
     grads_part = ug_sum[piece(q)].astype(F32)
     for k in range(NCHIP - 1):
@@ -300,23 +318,6 @@
         )
     expect("grx", grx, g_r.at[0])
     expect("grx sent", grx, g_s.at[0])
-
-    settle("go")
-    product = jnp.zeros((RB, GRADS), F32)
-    for part in range(2):
-        settle(("uz", part))
-        value = plane[part]
-        for k in range(NZ - 1):
-            value = value + uz[part, k].astype(F32)
-        product = product + jnp.dot(
-            value.astype(BF16), go[part * CH:(part + 1) * CH], preferred_element_type=F32
-        )
-    ftx[...] = product.astype(BF16)
-    slot = lax.rem(d, 4)
-    for j in range(4):
-        remote(ftx.at[:, pl.ds(128 * j, 256)], frx.at[slot], f_s.at[0], f_r.at[0], (4 * m + j, target))
-    expect("frx", frx, f_r.at[0])
-    expect("frx sent", frx, f_s.at[0])
 
     settle("br")
     base = bbuf[pl.ds(pl.multiple_of(m * OB, OB), OB)].astype(F32)

time: 38.6 us -> 38.4 us (level); the launches traced: 37.9 us -> 38.2 us
  no operation moved by 1% of the time
where the time goes in v5:
time: 38.4 us; the launch traced here: 38.2 us
  Pallas kernels  37.6 us (98%)
  local copies, waits for them, and re-layouts  0.61 us (2%)
    pallas_call x1, Pallas kernels, local(): pl.pallas_call(kernel, out_shape=pltpu.VMEM((OB, COLS), BF16), in_specs=[...  37.6 us

profile of v5, /device:TPU:7, one launch (start us, length us, event | category | flops | bytes accessed | tf_op | source)
XLA Modules:
  0.0 38.2 jit_solution(14592852461619478790)
XLA Ops:
  0.0 37.6 %shard_map.109 = bf16[32,160]{1,0:T(8,128)(2,1)S(1)} custom-call(bf16[128,3200]{1,0:T(8,128)(2,1)} %tk_h.1, bf16[128,640]{1,0:T(8,128)(2,1)} %tg_h.1, s32[1,128]{1,0:T(1,128)} %bitcast.9, bf16[3200,1024]{1,0:T(8,128)(2,1)} %kw_h.1, bf16[640,1024]{1,0:T(8,128)(2,1)} %gw_h.1, f32[1,1024]{1,0:T(1,128)} %bitcast.6, f32[1,1024]{1,0:T(1,128)} %bitcast.7, ...), custom_call_target="tpu_custom_call" | custom-call | flops 2000000000 | bytes 14000000 | tf_op jit(solution)/shard_map/pallas_call | solution.py:365
  37.6 0.6 %copy.13 = bf16[32,160]{1,0:T(8,128)(2,1)} copy(bf16[32,160]{1,0:T(8,128)(2,1)S(1)} %shard_map.109) | data formatting | bytes 20480

commit v6 on v5

--- a/solution.py
+++ b/solution.py
@@ -151,7 +151,8 @@
         pbuf[ch] = value.astype(BF16)
 
     def send_partial(first, many):
-        for k in (4, 3, 5, 2, 6, 1, 7):
+        for far in (4, 3, 5, 2, 6, 1, 7):
+            k = far + c * (NZ - 2 * far)
             to = lax.rem(m + k, NZ)
             rows = pl.ds(pl.multiple_of(to * TB, TB), TB)
             remote(
@@ -284,7 +285,8 @@
             value = value + uh_rs[part, k].astype(F32)
         plane.append(value)
         uz_tx[part] = value.astype(BF16)
-        for k in (4, 3, 5, 2, 6, 1, 7):
+        for far in (4, 3, 5, 2, 6, 1, 7):
+            k = far + c * (NZ - 2 * far)
             remote(uz_tx.at[part], uz.at[part, k - 1], z_s.at[part], z_r.at[part], zdev(k))
         expect(("uz", part), uz.at[part], z_r.at[part])
         expect(("uz sent", part), uz.at[part], z_s.at[part])

time: 38.4 us -> 38.5 us (level)
  no operation moved by 1% of the time
where the time goes in v6:
time: 38.5 us; the launch traced here: 38.2 us
  Pallas kernels  37.6 us (98%)
  local copies, waits for them, and re-layouts  0.61 us (2%)
    pallas_call x1, Pallas kernels, local(): pl.pallas_call(kernel, out_shape=pltpu.VMEM((OB, COLS), BF16), in_specs=[...  37.6 us

profile of v6, /device:TPU:7, one launch (start us, length us, event | category | flops | bytes accessed | tf_op | source)
XLA Modules:
  0.0 38.2 jit_solution(798928327727978027)
XLA Ops:
  0.0 37.6 %shard_map.109 = bf16[32,160]{1,0:T(8,128)(2,1)S(1)} custom-call(bf16[128,3200]{1,0:T(8,128)(2,1)} %tk_h.1, bf16[128,640]{1,0:T(8,128)(2,1)} %tg_h.1, s32[1,128]{1,0:T(1,128)} %bitcast.9, bf16[3200,1024]{1,0:T(8,128)(2,1)} %kw_h.1, bf16[640,1024]{1,0:T(8,128)(2,1)} %gw_h.1, f32[1,1024]{1,0:T(1,128)} %bitcast.6, f32[1,1024]{1,0:T(1,128)} %bitcast.7, ...), custom_call_target="tpu_custom_call" | custom-call | flops 2000000000 | bytes 14000000 | tf_op jit(solution)/shard_map/pallas_call | solution.py:367
  37.6 0.6 %copy.13 = bf16[32,160]{1,0:T(8,128)(2,1)} copy(bf16[32,160]{1,0:T(8,128)(2,1)S(1)} %shard_map.109) | data formatting | bytes 20480
